TPU v7x, 32 devices: a whole 2x2x4 slice. The times are simulated.
32 devices in a mesh: groups: 2 (over y), seq: 4 (over z), dp: 2 (over x), tensor: 2 (over core).
Axes of the slice: x: 2, y: 2, z: 4, core: 2. Of those that a mesh axis runs over, the one named last changes fastest.
Arguments:
- queries: bfloat16 [4, 768, 1024], P(('groups', 'dp'), 'seq', 'tensor'), parts along dimension 0, may hold values from -80 to 80
- key_rows: bfloat16 [4, 768, 1024], P(('groups', 'dp'), 'seq', 'tensor'), parts along dimension 0, may hold values from -80 to 80
- value_rows: bfloat16 [4, 768, 1024], P(('groups', 'dp'), 'seq', 'tensor'), parts along dimension 0, may hold values from -6 to 6
- utterance: int32 [4, 768], P(('groups', 'dp'), 'seq'), parts along dimension 0, may hold values from 0 to 7, never falling along the last dimension, each value on 1 to 576 neighbouring positions
- cotangent: bfloat16 [4, 768, 1024], P(('groups', 'dp'), 'seq'), parts along dimension 0, may hold values from -6 to 6
- out_weight: bfloat16 [1024, 1024], P('tensor'), may hold values from -0.1875 to 0.1875
Outputs:
- grad_queries: bfloat16 [4, 768, 1024], P(('groups', 'dp'), 'seq', 'tensor'), parts along dimension 0
- grad_keys: bfloat16 [4, 768, 1024], P(('groups', 'dp'), 'seq', 'tensor'), parts along dimension 0
- grad_values: bfloat16 [4, 768, 1024], P(('groups', 'dp'), 'seq', 'tensor'), parts along dimension 0
- grad_out_weight: float32 [2048, 1024], P(('groups', 'tensor')), parts along dimension 0
There are 2 independent parts, one for each index of `groups`. A program takes and returns all parts, laid end to end along the dimension named above; an argument that names none is the same for every part. Nothing has to cross between parts.
Inputs may be any that keep to these rules, and one draw needn't show every extreme that they name: Within each packed sequence utterance numbers never fall, all 8 occur, each utterance spans 1 to 576 frames and one spans exactly 576.
All inputs are finite; a program needn't handle non-finite values.
Results may differ from a plain program's by a relative error of at most 0.02.
Values may be sent and summed in bfloat16 or wider, within the bound.
A program may use at most 128 MiB of HBM per device.

v0:
```python
import math

import jax
import jax.numpy as jnp
from jax import lax
from jax.sharding import PartitionSpec as P

HD = 64


MASKED_SCORE = -1e30


def heads_of(array):
    return array.reshape(array.shape[0], array.shape[1] // HD, HD)


def block_scores(query_block, key_block, query_utts, key_utts):
    scores = jnp.einsum(
        "qhd,khd->hqk", query_block, key_block, preferred_element_type=jnp.float32
    ) * HD ** (-0.5)
    same_utt = query_utts[:, None] == key_utts[None, :]
    return jnp.where(same_utt[None], scores, MASKED_SCORE)


def score_gradient(probs, dout_block, value_block, delta_rows):
    prob_grads = jnp.einsum(
        "qhd,khd->hqk", dout_block, value_block, preferred_element_type=jnp.float32
    )
    return (probs * (prob_grads - delta_rows[:, :, None]) * HD ** (-0.5)).astype(jnp.bfloat16)


def local(queries, key_rows, value_rows, utterance, cotangent, out_weight):
    own_queries = queries[0]
    frames_dev = own_queries.shape[0]
    width_dev = own_queries.shape[1]
    heads_dev = width_dev // HD
    query_heads = heads_of(own_queries)
    my_utts = utterance[0]
    utts_all = lax.all_gather(my_utts, "seq", axis=0, tiled=True)
    keys_all, values_all = (
        lax.all_gather(key_rows[0], "seq", axis=0, tiled=True),
        lax.all_gather(value_rows[0], "seq", axis=0, tiled=True),
    )
    frames_all = keys_all.shape[0]
    key_span = math.gcd(frames_all, 512)
    block_count = frames_all // key_span

    def key_block(block_index):
        offset = block_index * key_span
        key_block_rows = heads_of(lax.dynamic_slice_in_dim(keys_all, offset, key_span, 0))
        value_block_rows = heads_of(lax.dynamic_slice_in_dim(values_all, offset, key_span, 0))
        utt_block = lax.dynamic_slice_in_dim(utts_all, offset, key_span, 0)
        return (key_block_rows, value_block_rows, utt_block)

    def stats_step(block_index, carried):
        key_block_rows, value_block_rows, utt_block = key_block(block_index)
        running_max, running_sum = carried
        scores = block_scores(query_heads, key_block_rows, my_utts, utt_block)
        new_max = jnp.maximum(running_max, jnp.max(scores, axis=2))
        running_sum = running_sum * jnp.exp(running_max - new_max) + jnp.sum(
            jnp.exp(scores - new_max[:, :, None]), axis=2
        )
        return (new_max, running_sum)

    start_max = jnp.full((heads_dev, frames_dev), MASKED_SCORE, jnp.float32)
    start_sum = jnp.zeros((heads_dev, frames_dev), jnp.float32)
    running_max, running_sum = lax.fori_loop(0, block_count, stats_step, (start_max, start_sum))
    log_norm = running_max + jnp.log(running_sum)

    def output_step(block_index, carried):
        key_block_rows, value_block_rows, utt_block = key_block(block_index)
        scores = block_scores(query_heads, key_block_rows, my_utts, utt_block)
        probs_low = jnp.exp(scores - log_norm[:, :, None]).astype(jnp.bfloat16)
        return carried + jnp.einsum(
            "hqk,khd->hqd", probs_low, value_block_rows, preferred_element_type=jnp.float32
        )

    head_zeros = jnp.zeros((heads_dev, frames_dev, HD), jnp.float32)
    attended_acc = lax.fori_loop(0, block_count, output_step, head_zeros)
    attended = attended_acc.transpose(1, 0, 2).reshape(frames_dev, width_dev).astype(jnp.bfloat16)
    own_cot = cotangent[0]
    d_attended = lax.dot_general(
        own_cot, out_weight, (((1,), (1,)), ((), ())), preferred_element_type=jnp.float32
    ).astype(jnp.bfloat16)
    weight_term = lax.dot_general(
        attended, own_cot, (((0,), (0,)), ((), ())), preferred_element_type=jnp.float32
    )
    grad_weight = lax.psum(weight_term, ("seq", "dp"))
    dout_heads = heads_of(d_attended)
    row_delta = jnp.einsum(
        "qhd,qhd->hq", dout_heads.astype(jnp.float32), heads_of(attended).astype(jnp.float32)
    )

    def joint_step(block_index, carried):
        key_block_rows, value_block_rows, utt_block = key_block(block_index)
        query_acc_now, buffer = carried
        scores = block_scores(query_heads, key_block_rows, my_utts, utt_block)
        probs = jnp.exp(scores - log_norm[:, :, None])
        score_grads = score_gradient(probs, dout_heads, value_block_rows, row_delta)
        query_acc_now = query_acc_now + jnp.einsum(
            "hqk,khd->hqd", score_grads, key_block_rows, preferred_element_type=jnp.float32
        )
        key_part = jnp.einsum(
            "hqk,qhd->khd", score_grads, query_heads, preferred_element_type=jnp.float32
        )
        value_part = jnp.einsum(
            "hqk,qhd->khd",
            probs.astype(jnp.bfloat16),
            dout_heads,
            preferred_element_type=jnp.float32,
        )
        joined = jnp.concatenate(
            [key_part.reshape(key_span, width_dev), value_part.reshape(key_span, width_dev)], axis=1
        )
        buffer = lax.dynamic_update_slice_in_dim(buffer, joined, block_index * key_span, 0)
        return (query_acc_now, buffer)

    term_zeros = jnp.zeros((frames_all, 2 * width_dev), jnp.float32)
    query_acc, terms_all = lax.fori_loop(0, block_count, joint_step, (head_zeros, term_zeros))
    summed = lax.psum_scatter(terms_all, "seq", scatter_dimension=0, tiled=True)
    grad_key = summed[:, :width_dev].astype(jnp.bfloat16)
    grad_value = summed[:, width_dev:].astype(jnp.bfloat16)
    grad_query = query_acc.transpose(1, 0, 2).reshape(frames_dev, width_dev).astype(jnp.bfloat16)
    return (grad_query[None], grad_key[None], grad_value[None], grad_weight)


def solution(mesh):
    placed = (
        P(("groups", "dp"), "seq", "tensor"),
        P(("groups", "dp"), "seq", "tensor"),
        P(("groups", "dp"), "seq", "tensor"),
        P(("groups", "dp"), "seq"),
        P(("groups", "dp"), "seq", None),
        P("tensor", None),
    )
    return jax.shard_map(
        local,
        mesh=mesh,
        in_specs=placed,
        out_specs=(
            P(("groups", "dp"), "seq", "tensor"),
            P(("groups", "dp"), "seq", "tensor"),
            P(("groups", "dp"), "seq", "tensor"),
            P(("groups", "tensor"), None),
        ),
        check_vma=False,
    )
```

profile of v0, /device:TPU:0, one launch (start us, length us, event | category | flops | bytes accessed | tf_op | source)
XLA Modules:
  0.0 269.7 jit_solution(2575673276808037903)
XLA Ops:
  8.1 1.3 dynamic-slice
  11.0 9.9 %all-reduce = s32[768]{0:T(1024)S(1)} all-reduce(s32[768]{0:T(1024)S(1)} %dynamic-update-slice), channel_id=2, replica_groups=mesh['groups'=2,'seq'=4,'dp'=2,'tensor'=2] {'seq'}, use_global_device_ids=true, to_apply=%add | all-reduce | flops 768 | bytes 6144 | tf_op jit(solution)/shard_map/all_gather | solution.py:40
  20.9 18.1 %all-gather.1 = bf16[1,768,512]{2,1,0:T(8,128)(2,1)S(1)} all-gather(bf16[1,192,512]{2,1,0:T(8,128)(2,1)} %param.13), channel_id=3, replica_groups=mesh['groups'=2,'seq'=4,'dp'=2,'tensor'=2] {'seq'}, dimensions={1}, use_global_device_ids=true | all-gather | bytes 983040 | tf_op jit(solution)/shard_map/all_gather | solution.py:42
  39.0 1.2 copy.30
  40.3 7.3 %while.46 = (s32[]{:T(128)}, f32[8,192]{1,0:T(8,128)S(1)}, f32[8,192]{1,0:T(8,128)S(1)}, s32[1,192]{1,0:T(1,128)S(1)}, s32[768]{0:T(1024)S(1)}, /*index=5*/bf16[...) while((s32[]{:T(128)}, f32[8,192]{1,0:T(8,128)S(1)}, ...), condition=%wide.region_3.4_spmd.clone, body=%wide.region_0.3_spmd.clone.sunk | while | flops 52354564 | bytes 4310966 | solution.py:68
  47.6 17.9 %all-gather.2 = bf16[1,768,512]{2,1,0:T(8,128)(2,1)S(1)} all-gather(bf16[1,192,512]{2,1,0:T(8,128)(2,1)} %param.14), channel_id=4, replica_groups=mesh['groups'=2,'seq'=4,'dp'=2,'tensor'=2] {'seq'}, dimensions={1}, use_global_device_ids=true | all-gather | bytes 983040 | tf_op jit(solution)/shard_map/all_gather | solution.py:43
  65.4 1.2 copy.31
  68.0 6.3 %while.47 = (s32[]{:T(128)}, f32[8,192,64]{1,2,0:T(8,128)S(1)}, s32[1,192]{1,0:T(1,128)S(1)}, s32[768]{0:T(1024)S(1)}, bf16[768,512]{0,1:T(8,128)(2,1)}, /*index...) while((s32[]{:T(128)}, f32[8,192,64]{1,2,0:T(8,128)S(1)}, ...), condition=%wide.region_5.6_spmd.clone, body=%wide.region_4.5_spmd.clone.sunk | while | flops 102481928 | bytes 2664381 | solution.py:80
  74.3 1.7 fusion.18
  76.0 2.0 broadcast_in_dim.120.clone
  78.1 28.6 %while.48 = (s32[]{:T(128)}, f32[8,192,64]{1,2,0:T(8,128)}, f32[768,1024]{1,0:T(8,128)}, s32[1,192]{1,0:T(1,128)S(1)}, s32[768]{0:T(1024)S(1)}, /*index=5*/bf16[...) while((s32[]{:T(128)}, f32[8,192,64]{1,2,0:T(8,128)}, ...), condition=%wide.region_7.8_spmd.clone, body=%wide.region_6.7_spmd.clone.sunk | while | flops 255311872 | bytes 20561964 | solution.py:120
  78.1 1.2 constant_dynamic-slice_fusion.10
  80.0 1.4 fusion.81
  81.4 2.1 convolution_add_fusion.2
  83.5 1.2 fusion.82
  84.8 1.2 fusion.83
  87.4 1.2 constant_dynamic-slice_fusion.10
  89.4 1.4 fusion.81
  90.8 2.3 convolution_add_fusion.2
  93.1 1.2 fusion.82
  94.3 1.2 fusion.83
  95.9 1.1 constant_dynamic-update-slice_fusion.2
  97.1 1.2 constant_dynamic-slice_fusion.10
  99.0 1.4 fusion.81
  100.4 2.3 convolution_add_fusion.2
  102.7 1.2 fusion.82
  103.9 1.2 fusion.83
  107.7 1.7 fusion.19
  111.4 69.4 %reduce-scatter.2.cloned.1.call-done = f32[192,1024]{1,0:T(8,128)} async-done(((f32[768,1024]{1,0:T(8,128)}), f32[192,1024]{1,0:T(8,128)}) %reduce-scatter.2.cloned.1.call-update) | async-done | bytes 786448 | tf_op jit(solution)/shard_map/reduce_scatter | solution.py:121
  180.8 1.2 convert.4
  182.7 76.3 %all-reduce.3.cloned.1.call-done = f32[512,1024]{1,0:T(8,128)} async-done(((f32[512,1024]{1,0:T(8,128)}), f32[512,1024]{1,0:T(8,128)}) %all-reduce.3.cloned.1.call-update) | async-done | bytes 2097168 | tf_op jit(solution)/shard_map/psum | solution.py:89
  259.1 3.2 %copy.74 = f32[512,1024]{1,0:T(8,128)} copy(f32[512,1024]{1,0:T(8,128)} %all-reduce.3.cloned.1.call-done) | data formatting | bytes 4194304
  (102 shorter events, 25.0 us)
Async XLA Ops:
  8.0 58.6 %copy-start = (bf16[512,1024]{1,0:T(8,128)(2,1)S(1)}, bf16[512,1024]{1,0:T(8,128)(2,1)}, u32[]{:S(2)}) copy-start(bf16[512,1024]{1,0:T(8,128)(2,1)} %param.17) | copy-start | bytes 3145732
  8.0 32.2 %copy-start.8 = (s32[1,192]{1,0:T(1,128)S(1)}, s32[1,192]{1,0:T(1,128)}, u32[]{:S(2)}) copy-start(s32[1,192]{1,0:T(1,128)} %param.15) | copy-start | bytes 2308
  8.0 32.1 %copy-start.9 = (bf16[1,192,512]{2,1,0:T(8,128)(2,1)S(1)}, bf16[1,192,512]{2,1,0:T(8,128)(2,1)}, u32[]{:S(2)}) copy-start(bf16[1,192,512]{2,1,0:T(8,128)(2,1)} %param.12) | copy-start | bytes 589828
  8.0 172.8 %reduce-scatter.2.cloned.1.call-start = ((), (), s32[]{:S(2)}) async-start(), calls=%async_computation.1 | async-start | bytes 3932160 | tf_op jit(solution)/shard_map/reduce_scatter | solution.py:121
  47.6 19.0 %copy-start.5 = (bf16[1,192,1024]{2,1,0:T(8,128)(2,1)S(1)}, bf16[1,192,1024]{2,1,0:T(8,128)(2,1)}, u32[]{:S(2)}) copy-start(bf16[1,192,1024]{2,1,0:T(8,128)(2,1)} %param.16) | copy-start | bytes 1179652
  78.1 1.9 copy-start.1
  79.2 0.8 copy-start.3
  86.4 1.1 copy-start.2
  87.4 1.9 copy-start.1
  88.6 0.8 copy-start.3
  95.9 1.1 copy-start.2
  97.1 1.9 copy-start.1
  98.2 0.8 copy-start.3
  105.6 1.1 copy-start.2
  106.7 1.0 copy-start.6
  106.7 1.1 copy-start.7
  106.7 152.4 %all-reduce.3.cloned.1.call-start = ((), (), s32[]{:S(2)}) async-start(), calls=%async_computation.2 | async-start | bytes 4194304 | tf_op jit(solution)/shard_map/psum | solution.py:89
  109.5 1.0 copy-start.4
Sparse Core Ops, SparseCore 0:
  106.8 73.9 reduce-scatter.1
Sparse Core Ops, SparseCore 1:
  111.4 147.7 all-reduce.2
where the time goes:
time: 271 us; the launch traced here: 270 us
  waiting for transfers between devices  146 us (54%)
  blocking collectives  45.8 us (17%)
  local copies, waits for them, and re-layouts  28.9 us (11%)
  matrix products  26.4 us (10%)
  between operations  16.3 us (6%)
  other arithmetic  5.89 us (2%)
    psum x1, waiting for transfers between devices, local(): grad_weight = lax.psum(weight_term, ('seq', 'dp'))  76.3 us
    reduce_scatter x1, waiting for transfers between devices, local(): summed = lax.psum_scatter(terms_all, 'seq', scatter_dimension=0, tiled=True)  69.4 us
    all_gather x1, blocking collectives, local(): lax.all_gather(key_rows[0], 'seq', axis=0, tiled=True)  18.1 us
    all_gather x1, blocking collectives, local(): lax.all_gather(value_rows[0], 'seq', axis=0, tiled=True)  17.9 us
    unnamed x22, local copies, waits for them, and re-layouts  10.6 us
    all_gather x1, blocking collectives, local(): utts_all = lax.all_gather(my_utts, 'seq', axis=0, tiled=True)  9.89 us
    dot_general x3, matrix products, joint_step(): jnp.einsum('hqk,khd->hqd', score_grads, key_block_rows, preferred_element...  6.76 us
    dynamic_slice x6, local copies, waits for them, and re-layouts, key_block(): lax.dynamic_slice_in_dim(values_all, offset, key_span, 0)  6.7 us
  transfers between devices with their start and end apart: 2, of which 2 were waited for; matrix products, arithmetic and copies ran while one was open for 2% of the time, Pallas kernels for 0%

commit v1 on v0

--- a/solution.py
+++ b/solution.py
@@ -1,8 +1,11 @@
+import functools
 import math
 
 import jax
 import jax.numpy as jnp
 from jax import lax
+from jax.experimental import pallas as pl
+from jax.experimental.pallas import tpu as pltpu
 from jax.sharding import PartitionSpec as P
 
 HD = 64
@@ -125,7 +128,260 @@
     return (grad_query[None], grad_key[None], grad_value[None], grad_weight)
 
 
+PAIR = 2 * HD
+NT = (((1,), (1,)), ((), ()))
+TN = (((0,), (0,)), ((), ()))
+MESH = pl.DeviceIdType.MESH
+
+
+def dot(a, b, dims=(((1,), (0,)), ((), ()))):
+    return lax.dot_general(a, b, dims, preferred_element_type=jnp.float32)
+
+
+def fused_kernel(
+    n, q_ref, k_ref, v_ref, utt_ref, cot_ref, w_ref,
+    dq_ref, dk_ref, dv_ref, gw_ref,
+    q_all, k_all, v_all, utt_all, cot_all, utt_col, utt_row, probs_all, att_all, dout_all,
+    dq_all, dk_all, dv_all, dk_acc, dv_acc, gw_part, gw_send, gw_recv,
+    in_send, in_recv, cot_send, cot_recv, core_send, core_recv,
+    out_send, out_recv, pair_send, pair_recv, gz_send, gz_recv, gx_send, gx_recv,
+):
+    me = lax.axis_index("seq")
+    core = lax.axis_index("tensor")
+    side = lax.axis_index("dp")
+    rows = q_ref.shape[0]
+    depth = cot_ref.shape[1]
+    half = depth // 2
+    scale = HD ** -0.5
+
+    def peer(d):
+        return lax.rem(me + d, n)
+
+    def source(d):
+        return lax.rem(me + n - d, n)
+
+    def frames(s):
+        return pl.ds(pl.multiple_of(s * rows, rows), rows)
+
+    def pair(s):
+        return pl.ds(pl.multiple_of(s * PAIR, PAIR), PAIR)
+
+    def halfcols(s):
+        return pl.ds(pl.multiple_of(s * half, half), half)
+
+    def remote(src, dst, ssem, rsem, target):
+        return pltpu.make_async_remote_copy(
+            src_ref=src, dst_ref=dst, send_sem=ssem, recv_sem=rsem,
+            device_id=target, device_id_type=MESH,
+        )
+
+    barrier = pltpu.get_barrier_semaphore()
+    for d in range(1, n):
+        pl.semaphore_signal(barrier, inc=1, device_id={"seq": peer(d)}, device_id_type=MESH)
+    pl.semaphore_signal(barrier, inc=1, device_id={"tensor": 1 - core}, device_id_type=MESH)
+    pl.semaphore_signal(barrier, inc=1, device_id={"dp": 1 - side}, device_id_type=MESH)
+    pl.semaphore_wait(barrier, n + 1)
+
+    in_copies = []
+    for d in range(1, n):
+        to = {"seq": peer(d)}
+        cols = pair(peer(d))
+        in_copies.append(remote(utt_ref, utt_all.at[me], in_send.at[3, d], in_recv.at[3, d], to))
+        for t, (src, dst) in enumerate(((k_ref, k_all), (v_ref, v_all), (q_ref, q_all))):
+            in_copies.append(remote(
+                src.at[:, cols], dst.at[frames(me), :], in_send.at[t, d], in_recv.at[t, d], to))
+    for copy in in_copies:
+        copy.start()
+    cot_copies = []
+    for d in range(1, n):
+        cot_copies.append(remote(
+            cot_ref.at[:, halfcols(core)], cot_all.at[frames(me), halfcols(core)],
+            cot_send.at[d], cot_recv.at[d], {"seq": peer(d)}))
+        cot_copies[-1].start()
+
+    own = pair(me)
+    q_all[frames(me), :] = q_ref[:, own]
+    k_all[frames(me), :] = k_ref[:, own]
+    v_all[frames(me), :] = v_ref[:, own]
+    cot_all[frames(me), :] = cot_ref[...]
+    utt_all[me] = utt_ref[...]
+    for copy in in_copies:
+        copy.wait_recv()
+
+    for s in range(n):
+        wide = jnp.broadcast_to(utt_all[s, 0:1, :], (128, utt_all.shape[2]))
+        utt_col[s * rows:(s + 1) * rows, :] = jnp.transpose(wide)[:rows, :]
+    utt_row[...] = jnp.transpose(utt_col[...])[0:8, :]
+
+    lane = lax.broadcasted_iota(jnp.int32, (rows, PAIR), 1)
+    first = lane < HD
+    masks = [first.astype(jnp.float32), (lane >= HD).astype(jnp.float32)]
+    masks_low = [m.astype(jnp.bfloat16) for m in masks]
+
+    def forward(i, carry):
+        here = frames(i)
+        q = q_all[here, :]
+        same = utt_col[here, 0:1] == utt_row[0:1, :]
+        outs = []
+        for h in range(2):
+            scores = dot(q * masks_low[h], k_all[...], NT) * scale
+            scores = jnp.where(same, scores, MASKED_SCORE)
+            e = jnp.exp(scores - jnp.max(scores, axis=1, keepdims=True))
+            probs = e * (1.0 / jnp.sum(e, axis=1, keepdims=True))
+            probs_all[h, here, :] = probs
+            outs.append(dot(probs.astype(jnp.bfloat16), v_all[...]))
+        att_all[here, :] = jnp.where(first, outs[0], outs[1]).astype(jnp.bfloat16)
+        return carry
+
+    lax.fori_loop(0, n, forward, 0)
+
+    core_copies = []
+    for d in range(1, n):
+        cot_copies[d - 1].wait_recv()
+        block = cot_all.at[frames(source(d)), halfcols(core)]
+        core_copies.append(remote(
+            block, block, core_send.at[d], core_recv.at[d], {"tensor": 1 - core}))
+        core_copies[-1].start()
+    for copy in core_copies:
+        copy.wait_recv()
+
+    for c in range(2):
+        gw_part[c] = dot(att_all[...], cot_all[:, c * half:(c + 1) * half], TN)
+    gw_send[...] = gw_part[1 - side].astype(jnp.bfloat16)
+    pair_copy = remote(gw_send, gw_recv, pair_send, pair_recv, {"dp": 1 - side})
+    pair_copy.start()
+
+    def project(i, carry):
+        here = frames(i)
+        dout_all[here, :] = dot(cot_all[here, :], w_ref[own, :], NT).astype(jnp.bfloat16)
+        return carry
+
+    lax.fori_loop(0, n, project, 0)
+    dk_acc[...] = jnp.zeros_like(dk_acc)
+    dv_acc[...] = jnp.zeros_like(dv_acc)
+
+    def backward(i):
+        here = frames(i)
+        q = q_all[here, :]
+        dout = dout_all[here, :]
+        product = dout.astype(jnp.float32) * att_all[here, :].astype(jnp.float32)
+        parts = []
+        for h in range(2):
+            delta = jnp.sum(product * masks[h], axis=1, keepdims=True)
+            dout_h = dout * masks_low[h]
+            probs = probs_all[h, here, :]
+            grads = (probs * (dot(dout_h, v_all[...], NT) - delta) * scale).astype(jnp.bfloat16)
+            parts.append(dot(grads, k_all[...]))
+            dk_acc[...] += dot(q * masks_low[h], grads, TN)
+            dv_acc[...] += dot(dout_h, probs.astype(jnp.bfloat16), TN)
+        dq_all[here, :] = jnp.where(first, parts[0], parts[1]).astype(jnp.bfloat16)
+
+    out_copies = []
+    gz_copies = []
+    gx_copies = []
+
+    def pass_on(s, slot):
+        block = gw_ref.at[pair(s), halfcols(side)]
+        copy = remote(block, block, gx_send.at[slot], gx_recv.at[slot], {"dp": 1 - side})
+        copy.start()
+        gx_copies.append(copy)
+
+    def send_out(t, src, dst, d):
+        copy = remote(
+            src.at[frames(peer(d)), :], dst.at[:, own],
+            out_send.at[t, d], out_recv.at[t, d], {"seq": peer(d)})
+        copy.start()
+        out_copies.append(copy)
+
+    for step in range(n):
+        d = (step + 1) % n
+        backward(peer(d))
+        if d:
+            send_out(0, dq_all, dq_ref, d)
+        if step == 0:
+            pair_copy.wait_recv()
+            gw_ref[own, halfcols(side)] = (
+                gw_part[side] + gw_recv[...].astype(jnp.float32)).astype(jnp.bfloat16)
+            block = gw_ref.at[own, halfcols(side)]
+            for e in range(1, n):
+                copy = remote(block, block, gz_send.at[e], gz_recv.at[e], {"seq": peer(e)})
+                copy.start()
+                gz_copies.append(copy)
+            pass_on(me, 0)
+
+    dk_all[...] = jnp.transpose(dk_acc[...]).astype(jnp.bfloat16)
+    for d in range(1, n):
+        send_out(1, dk_all, dk_ref, d)
+    dv_all[...] = jnp.transpose(dv_acc[...]).astype(jnp.bfloat16)
+    for d in range(1, n):
+        send_out(2, dv_all, dv_ref, d)
+    dq_ref[:, own] = dq_all[frames(me), :]
+    dk_ref[:, own] = dk_all[frames(me), :]
+    dv_ref[:, own] = dv_all[frames(me), :]
+    for d in range(1, n):
+        gz_copies[d - 1].wait_recv()
+        pass_on(source(d), d)
+    for copy in gx_copies + out_copies:
+        copy.wait_recv()
+    for copy in in_copies + cot_copies + core_copies + [pair_copy] + gz_copies + gx_copies + out_copies:
+        copy.wait_send()
+
+
+def fused(n, queries, key_rows, value_rows, utterance, cotangent, out_weight):
+    rows, width = queries.shape[1:]
+    depth = cotangent.shape[2]
+    total = n * rows
+    wide = -(-rows // 128) * 128
+    utts = jnp.broadcast_to(
+        jnp.pad(utterance.astype(jnp.float32), ((0, 0), (0, wide - rows))), (8, wide))
+    low, full = jnp.bfloat16, jnp.float32
+    vmem = pl.BlockSpec(memory_space=pltpu.VMEM)
+    dma = pltpu.SemaphoreType.DMA
+    dq, dk, dv, gw = pl.pallas_call(
+        functools.partial(fused_kernel, n),
+        out_shape=[jax.ShapeDtypeStruct((rows, width), low)] * 3
+        + [jax.ShapeDtypeStruct((width, depth), low)],
+        in_specs=[vmem] * 6,
+        out_specs=[vmem] * 4,
+        scratch_shapes=[
+            pltpu.VMEM((total, PAIR), low),
+            pltpu.VMEM((total, PAIR), low),
+            pltpu.VMEM((total, PAIR), low),
+            pltpu.VMEM((n, 8, wide), full),
+            pltpu.VMEM((total, depth), low),
+            pltpu.VMEM((total, 128), full),
+            pltpu.VMEM((8, total), full),
+            pltpu.VMEM((2, total, total), full),
+            pltpu.VMEM((total, PAIR), low),
+            pltpu.VMEM((total, PAIR), low),
+            pltpu.VMEM((total, PAIR), low),
+            pltpu.VMEM((total, PAIR), low),
+            pltpu.VMEM((total, PAIR), low),
+            pltpu.VMEM((PAIR, total), full),
+            pltpu.VMEM((PAIR, total), full),
+            pltpu.VMEM((2, PAIR, depth // 2), full),
+            pltpu.VMEM((PAIR, depth // 2), low),
+            pltpu.VMEM((PAIR, depth // 2), low),
+            dma((4, n)), dma((4, n)), dma((n,)), dma((n,)), dma((n,)), dma((n,)),
+            dma((3, n)), dma((3, n)), dma, dma, dma((n,)), dma((n,)), dma((n,)), dma((n,)),
+        ],
+        compiler_params=pltpu.CompilerParams(
+            collective_id=0, has_side_effects=True, vmem_limit_bytes=40 << 20),
+    )(queries[0], key_rows[0], value_rows[0], utts, cotangent[0], out_weight)
+    return dq[None], dk[None], dv[None], gw.astype(full)
+
+
 def solution(mesh):
+    n = mesh.shape["seq"]
+
+    def body(*args):
+        width, rows = args[0].shape[2], args[0].shape[1]
+        fits = (
+            width == n * PAIR and rows % 16 == 0 and n > 1
+            and mesh.shape["dp"] == 2 and mesh.shape["tensor"] == 2
+        )
+        return fused(n, *args) if fits else local(*args)
+
     placed = (
         P(("groups", "dp"), "seq", "tensor"),
         P(("groups", "dp"), "seq", "tensor"),
@@ -135,7 +391,7 @@
         P("tensor", None),
     )
     return jax.shard_map(
-        local,
+        body,
         mesh=mesh,
         in_specs=placed,
         out_specs=(

time: 271 us -> 77.3 us (0.29)
  the two profiles are of different devices: /device:TPU:0 before, /device:TPU:18 now
where the time goes in v1:
time: 77.3 us; the launch traced here: 77 us
  Pallas kernels  67.1 us (87%)
  local copies, waits for them, and re-layouts  7.04 us (9%)
  other arithmetic  2.25 us (3%)
    pallas_call x1, Pallas kernels, fused(): pl.pallas_call(functools.partial(fused_kernel, n), out_shape=[jax.ShapeDt...  67.1 us
    unnamed x13, local copies, waits for them, and re-layouts  7.02 us
    convert_element_type x1, other arithmetic, fused(): return (dq[None], dk[None], dv[None], gw.astype(full))  1.57 us

profile of v1, /device:TPU:18, one launch (start us, length us, event | category | flops | bytes accessed | tf_op | source)
XLA Modules:
  0.0 77.0 jit_solution(2555143662619400998)
XLA Ops:
  0.6 0.7 convert_element_type.8
  1.3 0.0 copy-start
  1.3 1.2 %copy-done = bf16[512,1024]{1,0:T(8,128)(2,1)S(1)} copy-done((bf16[512,1024]{1,0:T(8,128)(2,1)S(1)}, bf16[512,1024]{1,0:T(8,128)(2,1)}, u32[]{:S(2)}) %copy-start) | copy-done | bytes 1048600
  2.6 0.0 copy-start.1
  2.6 1.0 %copy-done.1 = bf16[1,192,1024]{2,1,0:T(8,128)(2,1)S(1)} copy-done((bf16[1,192,1024]{2,1,0:T(8,128)(2,1)S(1)}, bf16[1,192,1024]{2,1,0:T(8,128)(2,1)}, u32[]{:S(2)}) %copy-start.1) | copy-done | bytes 393240
  3.5 0.0 copy-start.2
  3.6 0.9 %copy-done.2 = bf16[1,192,512]{2,1,0:T(8,128)(2,1)S(1)} copy-done((bf16[1,192,512]{2,1,0:T(8,128)(2,1)S(1)}, bf16[1,192,512]{2,1,0:T(8,128)(2,1)}, u32[]{:S(2)}) %copy-start.2) | copy-done | bytes 196632
  4.5 0.0 copy-start.3
  4.5 0.9 %copy-done.3 = bf16[1,192,512]{2,1,0:T(8,128)(2,1)S(1)} copy-done((bf16[1,192,512]{2,1,0:T(8,128)(2,1)S(1)}, bf16[1,192,512]{2,1,0:T(8,128)(2,1)}, u32[]{:S(2)}) %copy-start.3) | copy-done | bytes 196632
  5.4 0.0 copy-start.4
  5.4 0.9 %copy-done.4 = bf16[1,192,512]{2,1,0:T(8,128)(2,1)S(1)} copy-done((bf16[1,192,512]{2,1,0:T(8,128)(2,1)S(1)}, bf16[1,192,512]{2,1,0:T(8,128)(2,1)}, u32[]{:S(2)}) %copy-start.4) | copy-done | bytes 196632
  6.3 67.1 %shard_map.93 = (bf16[192,512]{1,0:T(8,128)(2,1)S(1)}, bf16[192,512]{1,0:T(8,128)(2,1)S(1)}, bf16[192,512]{1,0:T(8,128)(2,1)S(1)}, bf16[512,1024]{1,0:T(8,128)(2,1)S(1)}) custom-call(bf16[192,512]{1,0:T(8,128)(2,1)S(1)} %bitcast.12, bf16[192,512]{1,0:T(8,128)(2,1)S(1)} %bitcast.13, bf16[192,512]{1,0:T(8,128)(2,1)S(1)} %bitcast.14, ...), custom_call_target="tpu_custom_call" | custom-call | tf_op jit(solution)/shard_map/pallas_call | solution.py:340
  73.4 1.6 %convert_element_type.9 = f32[512,1024]{1,0:T(8,128)} convert(bf16[512,1024]{1,0:T(8,128)(2,1)S(1)} %get-tuple-element.11) | non-fusion elementwise | flops 524288 | bytes 3145728 | tf_op jit(solution)/shard_map/convert_element_type | solution.py:371
  75.0 0.7 copy.13
  75.7 0.7 copy.14
  76.3 0.7 copy.15
  (2 shorter events, 0.0 us)
Async XLA Ops:
  1.3 1.2 %copy-start = (bf16[512,1024]{1,0:T(8,128)(2,1)S(1)}, bf16[512,1024]{1,0:T(8,128)(2,1)}, u32[]{:S(2)}) copy-start(bf16[512,1024]{1,0:T(8,128)(2,1)} %w_ref.1) | copy-start | bytes 3145732
  2.6 1.0 %copy-start.1 = (bf16[1,192,1024]{2,1,0:T(8,128)(2,1)S(1)}, bf16[1,192,1024]{2,1,0:T(8,128)(2,1)}, u32[]{:S(2)}) copy-start(bf16[1,192,1024]{2,1,0:T(8,128)(2,1)} %param.10) | copy-start | bytes 1179652
  3.5 0.9 %copy-start.2 = (bf16[1,192,512]{2,1,0:T(8,128)(2,1)S(1)}, bf16[1,192,512]{2,1,0:T(8,128)(2,1)}, u32[]{:S(2)}) copy-start(bf16[1,192,512]{2,1,0:T(8,128)(2,1)} %param.6) | copy-start | bytes 589828
  4.5 0.9 %copy-start.3 = (bf16[1,192,512]{2,1,0:T(8,128)(2,1)S(1)}, bf16[1,192,512]{2,1,0:T(8,128)(2,1)}, u32[]{:S(2)}) copy-start(bf16[1,192,512]{2,1,0:T(8,128)(2,1)} %param.7) | copy-start | bytes 589828
  5.4 0.9 %copy-start.4 = (bf16[1,192,512]{2,1,0:T(8,128)(2,1)S(1)}, bf16[1,192,512]{2,1,0:T(8,128)(2,1)}, u32[]{:S(2)}) copy-start(bf16[1,192,512]{2,1,0:T(8,128)(2,1)} %param.8) | copy-start | bytes 589828

commit v2 on v1

--- a/solution.py
+++ b/solution.py
@@ -132,6 +132,7 @@
 NT = (((1,), (1,)), ((), ()))
 TN = (((0,), (0,)), ((), ()))
 MESH = pl.DeviceIdType.MESH
+CUTS = 2
 
 
 def dot(a, b, dims=(((1,), (0,)), ((), ()))):
@@ -141,33 +142,29 @@
 def fused_kernel(
     n, q_ref, k_ref, v_ref, utt_ref, cot_ref, w_ref,
     dq_ref, dk_ref, dv_ref, gw_ref,
-    q_all, k_all, v_all, utt_all, cot_all, utt_col, utt_row, probs_all, att_all, dout_all,
+    q_all, k_all, v_all, utt_pad, utt_all, cot_all, w_own, utt_col, utt_row, probs_all, att_all,
     dq_all, dk_all, dv_all, dk_acc, dv_acc, gw_part, gw_send, gw_recv,
-    in_send, in_recv, cot_send, cot_recv, core_send, core_recv,
+    local_sem, in_send, in_recv, cot_send, cot_recv, core_send, core_recv,
     out_send, out_recv, pair_send, pair_recv, gz_send, gz_recv, gx_send, gx_recv,
 ):
     me = lax.axis_index("seq")
     core = lax.axis_index("tensor")
     side = lax.axis_index("dp")
     rows = q_ref.shape[0]
-    depth = cot_ref.shape[1]
-    half = depth // 2
     scale = HD ** -0.5
 
     def peer(d):
         return lax.rem(me + d, n)
 
-    def source(d):
-        return lax.rem(me + n - d, n)
-
     def frames(s):
         return pl.ds(pl.multiple_of(s * rows, rows), rows)
 
     def pair(s):
         return pl.ds(pl.multiple_of(s * PAIR, PAIR), PAIR)
 
-    def halfcols(s):
-        return pl.ds(pl.multiple_of(s * half, half), half)
+    def slab(base, extent, who, cut):
+        size = extent // (2 * CUTS)
+        return pl.ds(pl.multiple_of(base + who * (extent // 2) + cut * size, size), size)
 
     def remote(src, dst, ssem, rsem, target):
         return pltpu.make_async_remote_copy(
@@ -180,31 +177,65 @@
         pl.semaphore_signal(barrier, inc=1, device_id={"seq": peer(d)}, device_id_type=MESH)
     pl.semaphore_signal(barrier, inc=1, device_id={"tensor": 1 - core}, device_id_type=MESH)
     pl.semaphore_signal(barrier, inc=1, device_id={"dp": 1 - side}, device_id_type=MESH)
+
+    own = pair(me)
+    local_copies = [
+        pltpu.make_async_copy(src, dst, local_sem.at[i])
+        for i, (src, dst) in enumerate((
+            (q_ref.at[:, own], q_all.at[frames(me), :]),
+            (k_ref.at[:, own], k_all.at[frames(me), :]),
+            (v_ref.at[:, own], v_all.at[frames(me), :]),
+            (cot_ref, cot_all.at[frames(me), :]),
+            (w_ref.at[own, :], w_own),
+        ))
+    ]
+    for copy in local_copies:
+        copy.start()
+    utt_pad[...] = jnp.zeros_like(utt_pad)
+    utt_pad[0:1, 0:rows] = utt_ref[...].astype(jnp.float32)
+    utt_all[me] = utt_pad[...]
+
+    order = [jnp.int32(0)] * (n - 1)
+    count = jnp.int32(0)
+    for dist in range(1, n):
+        for s in (me - dist, me + dist):
+            valid = jnp.logical_and(s >= 0, s < n)
+            for k in range(n - 1):
+                order[k] = jnp.where(jnp.logical_and(valid, count == k), s, order[k])
+            count = count + valid.astype(jnp.int32)
+
+    def onward(src, dst, s, cut, ssem, rsem, act):
+        @pl.when(jnp.logical_and(s <= me, me < n - 1))
+        def _():
+            act(remote(src, dst, ssem.at[0, s, cut], rsem.at[s, cut], {"seq": lax.rem(me + 1, n)}))
+
+        @pl.when(jnp.logical_and(s >= me, me > 0))
+        def _():
+            act(remote(src, dst, ssem.at[1, s, cut], rsem.at[s, cut], {"seq": lax.rem(me + n - 1, n)}))
+
+    start = lambda copy: copy.start()
+    wait_send = lambda copy: copy.wait_send()
+
     pl.semaphore_wait(barrier, n + 1)
-
     in_copies = []
     for d in range(1, n):
         to = {"seq": peer(d)}
         cols = pair(peer(d))
-        in_copies.append(remote(utt_ref, utt_all.at[me], in_send.at[3, d], in_recv.at[3, d], to))
+        in_copies.append(remote(utt_pad, utt_all.at[me], in_send.at[3, d], in_recv.at[3, d], to))
         for t, (src, dst) in enumerate(((k_ref, k_all), (v_ref, v_all), (q_ref, q_all))):
             in_copies.append(remote(
                 src.at[:, cols], dst.at[frames(me), :], in_send.at[t, d], in_recv.at[t, d], to))
     for copy in in_copies:
         copy.start()
-    cot_copies = []
-    for d in range(1, n):
-        cot_copies.append(remote(
-            cot_ref.at[:, halfcols(core)], cot_all.at[frames(me), halfcols(core)],
-            cot_send.at[d], cot_recv.at[d], {"seq": peer(d)}))
-        cot_copies[-1].start()
-
-    own = pair(me)
-    q_all[frames(me), :] = q_ref[:, own]
-    k_all[frames(me), :] = k_ref[:, own]
-    v_all[frames(me), :] = v_ref[:, own]
-    cot_all[frames(me), :] = cot_ref[...]
-    utt_all[me] = utt_ref[...]
+
+    def cot_block(s, cut):
+        return cot_all.at[slab(s * rows, rows, core, cut), :]
+
+    for cut in range(CUTS):
+        onward(cot_ref.at[slab(0, rows, core, cut), :], cot_block(me, cut), me, cut,
+               cot_send, cot_recv, start)
+    for copy in local_copies:
+        copy.wait()
     for copy in in_copies:
         copy.wait_recv()
 
@@ -218,7 +249,7 @@
     masks = [first.astype(jnp.float32), (lane >= HD).astype(jnp.float32)]
     masks_low = [m.astype(jnp.bfloat16) for m in masks]
 
-    def forward(i, carry):
+    def forward(i):
         here = frames(i)
         q = q_all[here, :]
         same = utt_col[here, 0:1] == utt_row[0:1, :]
@@ -231,39 +262,43 @@
             probs_all[h, here, :] = probs
             outs.append(dot(probs.astype(jnp.bfloat16), v_all[...]))
         att_all[here, :] = jnp.where(first, outs[0], outs[1]).astype(jnp.bfloat16)
+
+    def forward_step(i, carry):
+        forward(i)
         return carry
 
-    lax.fori_loop(0, n, forward, 0)
-
     core_copies = []
-    for d in range(1, n):
-        cot_copies[d - 1].wait_recv()
-        block = cot_all.at[frames(source(d)), halfcols(core)]
-        core_copies.append(remote(
-            block, block, core_send.at[d], core_recv.at[d], {"tensor": 1 - core}))
-        core_copies[-1].start()
-    for copy in core_copies:
-        copy.wait_recv()
-
-    for c in range(2):
-        gw_part[c] = dot(att_all[...], cot_all[:, c * half:(c + 1) * half], TN)
-    gw_send[...] = gw_part[1 - side].astype(jnp.bfloat16)
-    pair_copy = remote(gw_send, gw_recv, pair_send, pair_recv, {"dp": 1 - side})
-    pair_copy.start()
-
-    def project(i, carry):
-        here = frames(i)
-        dout_all[here, :] = dot(cot_all[here, :], w_ref[own, :], NT).astype(jnp.bfloat16)
-        return carry
-
-    lax.fori_loop(0, n, project, 0)
+
+    def take_cot(k):
+        s = order[k]
+        for cut in range(CUTS):
+            block = cot_block(s, cut)
+            copy = remote(
+                block, block, core_send.at[k, cut], core_recv.at[k, cut], {"tensor": 1 - core})
+            remote(block, block, core_send.at[k, cut], cot_recv.at[s, cut],
+                   {"tensor": 1 - core}).wait_recv()
+            onward(block, block, s, cut, cot_send, cot_recv, start)
+            copy.start()
+            core_copies.append(copy)
+
+    gw_part[...] = jnp.zeros_like(gw_part)
     dk_acc[...] = jnp.zeros_like(dk_acc)
     dv_acc[...] = jnp.zeros_like(dv_acc)
+    lax.fori_loop(0, n // 2, forward_step, 0)
+    take_cot(0)
+    lax.fori_loop(n // 2, n, forward_step, 0)
+
+    def slab_half(who):
+        return pl.ds(pl.multiple_of(who * HD, HD), HD)
+
+    def weigh(i):
+        here = frames(i)
+        gw_part[...] += dot(att_all[here, :], cot_all[here, :], TN)
 
     def backward(i):
         here = frames(i)
         q = q_all[here, :]
-        dout = dout_all[here, :]
+        dout = dot(cot_all[here, :], w_own[...], NT).astype(jnp.bfloat16)
         product = dout.astype(jnp.float32) * att_all[here, :].astype(jnp.float32)
         parts = []
         for h in range(2):
@@ -277,53 +312,74 @@
         dq_all[here, :] = jnp.where(first, parts[0], parts[1]).astype(jnp.bfloat16)
 
     out_copies = []
-    gz_copies = []
+
+    def send_out(t, src, dst, to):
+        d = lax.rem(to - me + n, n)
+        copy = remote(
+            src.at[frames(to), :], dst.at[:, own],
+            out_send.at[t, d], out_recv.at[t, d], {"seq": to})
+        copy.start()
+        out_copies.append(copy)
+
+    weigh(me)
+    backward(me)
+    for k in range(n - 1):
+        if k:
+            take_cot(k)
+        for copy in core_copies[k * CUTS:(k + 1) * CUTS]:
+            copy.wait_recv()
+        weigh(order[k])
+        if k == n - 2:
+            gw_send[...] = gw_part[slab_half(1 - side), :].astype(jnp.bfloat16)
+            pair_copy = remote(gw_send, gw_recv, pair_send, pair_recv, {"dp": 1 - side})
+            pair_copy.start()
+        backward(order[k])
+        send_out(0, dq_all, dq_ref, order[k])
+
+    dk_all[...] = jnp.transpose(dk_acc[...]).astype(jnp.bfloat16)
+    dv_all[...] = jnp.transpose(dv_acc[...]).astype(jnp.bfloat16)
+
     gx_copies = []
 
-    def pass_on(s, slot):
-        block = gw_ref.at[pair(s), halfcols(side)]
-        copy = remote(block, block, gx_send.at[slot], gx_recv.at[slot], {"dp": 1 - side})
+    def gw_block(s, cut):
+        return gw_ref.at[slab(s * PAIR, PAIR, side, cut), :]
+
+    def pass_on(s, slot, cut):
+        block = gw_block(s, cut)
+        copy = remote(
+            block, block, gx_send.at[slot, cut], gx_recv.at[slot, cut], {"dp": 1 - side})
         copy.start()
         gx_copies.append(copy)
 
-    def send_out(t, src, dst, d):
-        copy = remote(
-            src.at[frames(peer(d)), :], dst.at[:, own],
-            out_send.at[t, d], out_recv.at[t, d], {"seq": peer(d)})
-        copy.start()
-        out_copies.append(copy)
-
-    for step in range(n):
-        d = (step + 1) % n
-        backward(peer(d))
-        if d:
-            send_out(0, dq_all, dq_ref, d)
-        if step == 0:
-            pair_copy.wait_recv()
-            gw_ref[own, halfcols(side)] = (
-                gw_part[side] + gw_recv[...].astype(jnp.float32)).astype(jnp.bfloat16)
-            block = gw_ref.at[own, halfcols(side)]
-            for e in range(1, n):
-                copy = remote(block, block, gz_send.at[e], gz_recv.at[e], {"seq": peer(e)})
-                copy.start()
-                gz_copies.append(copy)
-            pass_on(me, 0)
-
-    dk_all[...] = jnp.transpose(dk_acc[...]).astype(jnp.bfloat16)
-    for d in range(1, n):
-        send_out(1, dk_all, dk_ref, d)
-    dv_all[...] = jnp.transpose(dv_acc[...]).astype(jnp.bfloat16)
-    for d in range(1, n):
-        send_out(2, dv_all, dv_ref, d)
+    pair_copy.wait_recv()
+    gw_ref[pl.ds(pl.multiple_of(me * PAIR + side * HD, HD), HD), :] = (
+        gw_part[slab_half(side), :] + gw_recv[...].astype(jnp.float32)).astype(jnp.bfloat16)
+    for cut in range(CUTS):
+        onward(gw_block(me, cut), gw_block(me, cut), me, cut, gz_send, gz_recv, start)
+    for cut in range(CUTS):
+        pass_on(me, n - 1, cut)
+    for t, (src, dst) in ((1, (dk_all, dk_ref)), (2, (dv_all, dv_ref))):
+        for d in range(1, n):
+            send_out(t, src, dst, peer(d))
     dq_ref[:, own] = dq_all[frames(me), :]
     dk_ref[:, own] = dk_all[frames(me), :]
     dv_ref[:, own] = dv_all[frames(me), :]
-    for d in range(1, n):
-        gz_copies[d - 1].wait_recv()
-        pass_on(source(d), d)
+    for k in range(n - 1):
+        s = order[k]
+        for cut in range(CUTS):
+            block = gw_block(s, cut)
+            remote(block, block, gx_send.at[k, cut], gz_recv.at[s, cut],
+                   {"dp": 1 - side}).wait_recv()
+            onward(block, block, s, cut, gz_send, gz_recv, start)
+            pass_on(s, k, cut)
     for copy in gx_copies + out_copies:
         copy.wait_recv()
-    for copy in in_copies + cot_copies + core_copies + [pair_copy] + gz_copies + gx_copies + out_copies:
+    for s in [me] + order:
+        for cut in range(CUTS):
+            block, done = cot_block(s, cut), gw_block(s, cut)
+            onward(block, block, s, cut, cot_send, cot_recv, wait_send)
+            onward(done, done, s, cut, gz_send, gz_recv, wait_send)
+    for copy in in_copies + core_copies + [pair_copy] + gx_copies + out_copies:
         copy.wait_send()
 
 
@@ -332,23 +388,24 @@
     depth = cotangent.shape[2]
     total = n * rows
     wide = -(-rows // 128) * 128
-    utts = jnp.broadcast_to(
-        jnp.pad(utterance.astype(jnp.float32), ((0, 0), (0, wide - rows))), (8, wide))
     low, full = jnp.bfloat16, jnp.float32
     vmem = pl.BlockSpec(memory_space=pltpu.VMEM)
+    hbm = pl.BlockSpec(memory_space=pltpu.HBM)
     dma = pltpu.SemaphoreType.DMA
     dq, dk, dv, gw = pl.pallas_call(
         functools.partial(fused_kernel, n),
         out_shape=[jax.ShapeDtypeStruct((rows, width), low)] * 3
         + [jax.ShapeDtypeStruct((width, depth), low)],
-        in_specs=[vmem] * 6,
+        in_specs=[hbm, hbm, hbm, vmem, hbm, hbm],
         out_specs=[vmem] * 4,
         scratch_shapes=[
             pltpu.VMEM((total, PAIR), low),
             pltpu.VMEM((total, PAIR), low),
             pltpu.VMEM((total, PAIR), low),
+            pltpu.VMEM((8, wide), full),
             pltpu.VMEM((n, 8, wide), full),
             pltpu.VMEM((total, depth), low),
+            pltpu.VMEM((PAIR, depth), low),
             pltpu.VMEM((total, 128), full),
             pltpu.VMEM((8, total), full),
             pltpu.VMEM((2, total, total), full),
@@ -356,18 +413,18 @@
             pltpu.VMEM((total, PAIR), low),
             pltpu.VMEM((total, PAIR), low),
             pltpu.VMEM((total, PAIR), low),
-            pltpu.VMEM((total, PAIR), low),
             pltpu.VMEM((PAIR, total), full),
             pltpu.VMEM((PAIR, total), full),
-            pltpu.VMEM((2, PAIR, depth // 2), full),
-            pltpu.VMEM((PAIR, depth // 2), low),
-            pltpu.VMEM((PAIR, depth // 2), low),
-            dma((4, n)), dma((4, n)), dma((n,)), dma((n,)), dma((n,)), dma((n,)),
-            dma((3, n)), dma((3, n)), dma, dma, dma((n,)), dma((n,)), dma((n,)), dma((n,)),
+            pltpu.VMEM((PAIR, depth), full),
+            pltpu.VMEM((HD, depth), low),
+            pltpu.VMEM((HD, depth), low),
+            dma((5,)), dma((4, n)), dma((4, n)), dma((2, n, CUTS)), dma((n, CUTS)),
+            dma((n, CUTS)), dma((n, CUTS)), dma((3, n)), dma((3, n)), dma, dma,
+            dma((2, n, CUTS)), dma((n, CUTS)), dma((n, CUTS)), dma((n, CUTS)),
         ],
         compiler_params=pltpu.CompilerParams(
-            collective_id=0, has_side_effects=True, vmem_limit_bytes=40 << 20),
-    )(queries[0], key_rows[0], value_rows[0], utts, cotangent[0], out_weight)
+            collective_id=0, has_side_effects=True, vmem_limit_bytes=60 << 20),
+    )(queries[0], key_rows[0], value_rows[0], utterance, cotangent[0], out_weight)
     return dq[None], dk[None], dv[None], gw.astype(full)
 
 
@@ -377,7 +434,7 @@
     def body(*args):
         width, rows = args[0].shape[2], args[0].shape[1]
         fits = (
-            width == n * PAIR and rows % 16 == 0 and n > 1
+            width == n * PAIR and rows % (32 * CUTS) == 0 and n > 1
             and mesh.shape["dp"] == 2 and mesh.shape["tensor"] == 2
         )
         return fused(n, *args) if fits else local(*args)

time: 77.3 us -> 71.1 us (0.920)
  the two profiles are of different devices: /device:TPU:18 before, /device:TPU:0 now
where the time goes in v2:
time: 71.1 us; the launch traced here: 71 us
  Pallas kernels  65.4 us (92%)
  other arithmetic  2.85 us (4%)
  local copies, waits for them, and re-layouts  2.04 us (3%)
    pallas_call x1, Pallas kernels, fused(): pl.pallas_call(functools.partial(fused_kernel, n), out_shape=[jax.ShapeDt...  65.4 us
    convert_element_type x1, other arithmetic, fused(): return (dq[None], dk[None], dv[None], gw.astype(full))  2.85 us
    unnamed x9, local copies, waits for them, and re-layouts  2.04 us

profile of v2, /device:TPU:0, one launch (start us, length us, event | category | flops | bytes accessed | tf_op | source)
XLA Modules:
  0.0 71.0 jit_solution(6991709111246091861)
XLA Ops:
  0.6 65.4 %shard_map.93 = (bf16[192,512]{1,0:T(8,128)(2,1)}, bf16[192,512]{1,0:T(8,128)(2,1)}, bf16[192,512]{1,0:T(8,128)(2,1)}, bf16[512,1024]{1,0:T(8,128)(2,1)}) custom-call(bf16[192,512]{1,0:T(8,128)(2,1)} %bitcast.8, bf16[192,512]{1,0:T(8,128)(2,1)} %bitcast.9, bf16[192,512]{1,0:T(8,128)(2,1)} %bitcast.10, s32[1,192]{1,0:T(1,128)} %utt_ref.1, ...), custom_call_target="tpu_custom_call" | custom-call | tf_op jit(solution)/shard_map/pallas_call | solution.py:395
  66.1 0.0 copy-start.2
  66.1 0.0 copy-start.1
  66.1 0.0 copy-start
  66.1 2.8 %convert_element_type.3 = f32[512,1024]{1,0:T(8,128)} convert(bf16[512,1024]{1,0:T(8,128)(2,1)} %get-tuple-element.11) | non-fusion elementwise | flops 524288 | bytes 3145728 | tf_op jit(solution)/shard_map/convert_element_type | solution.py:428
  68.9 0.0 copy-done.2
  68.9 0.7 copy.13
  69.6 0.0 copy-done.1
  69.6 0.7 copy.14
  70.3 0.0 copy-done
  70.3 0.7 copy.15
Async XLA Ops:
  66.1 2.9 %copy-start.2 = (bf16[192,512]{1,0:T(8,128)(2,1)S(1)}, bf16[192,512]{1,0:T(8,128)(2,1)}, u32[]{:S(2)}) copy-start(bf16[192,512]{1,0:T(8,128)(2,1)} %get-tuple-element.8) | copy-start | bytes 589828
  66.1 3.6 %copy-start.1 = (bf16[192,512]{1,0:T(8,128)(2,1)S(1)}, bf16[192,512]{1,0:T(8,128)(2,1)}, u32[]{:S(2)}) copy-start(bf16[192,512]{1,0:T(8,128)(2,1)} %get-tuple-element.9) | copy-start | bytes 589828
  66.1 4.2 %copy-start = (bf16[192,512]{1,0:T(8,128)(2,1)S(1)}, bf16[192,512]{1,0:T(8,128)(2,1)}, u32[]{:S(2)}) copy-start(bf16[192,512]{1,0:T(8,128)(2,1)} %get-tuple-element.10) | copy-start | bytes 589828

commit v3 on v2

--- a/solution.py
+++ b/solution.py
@@ -225,8 +225,6 @@
         for t, (src, dst) in enumerate(((k_ref, k_all), (v_ref, v_all), (q_ref, q_all))):
             in_copies.append(remote(
                 src.at[:, cols], dst.at[frames(me), :], in_send.at[t, d], in_recv.at[t, d], to))
-    for copy in in_copies:
-        copy.start()
 
     def cot_block(s, cut):
         return cot_all.at[slab(s * rows, rows, core, cut), :]
@@ -234,8 +232,26 @@
     for cut in range(CUTS):
         onward(cot_ref.at[slab(0, rows, core, cut), :], cot_block(me, cut), me, cut,
                cot_send, cot_recv, start)
+    for copy in in_copies:
+        copy.start()
     for copy in local_copies:
         copy.wait()
+    core_copies = []
+
+    def take_cot(k):
+        s = order[k]
+        for cut in range(CUTS):
+            block = cot_block(s, cut)
+            copy = remote(
+                block, block, core_send.at[k, cut], core_recv.at[k, cut], {"tensor": 1 - core})
+            remote(block, block, core_send.at[k, cut], cot_recv.at[s, cut],
+                   {"tensor": 1 - core}).wait_recv()
+            onward(block, block, s, cut, cot_send, cot_recv, start)
+            copy.start()
+            core_copies.append(copy)
+
+    take_cot(0)
+    take_cot(1)
     for copy in in_copies:
         copy.wait_recv()
 
@@ -267,25 +283,10 @@
         forward(i)
         return carry
 
-    core_copies = []
-
-    def take_cot(k):
-        s = order[k]
-        for cut in range(CUTS):
-            block = cot_block(s, cut)
-            copy = remote(
-                block, block, core_send.at[k, cut], core_recv.at[k, cut], {"tensor": 1 - core})
-            remote(block, block, core_send.at[k, cut], cot_recv.at[s, cut],
-                   {"tensor": 1 - core}).wait_recv()
-            onward(block, block, s, cut, cot_send, cot_recv, start)
-            copy.start()
-            core_copies.append(copy)
-
     gw_part[...] = jnp.zeros_like(gw_part)
     dk_acc[...] = jnp.zeros_like(dk_acc)
     dv_acc[...] = jnp.zeros_like(dv_acc)
     lax.fori_loop(0, n // 2, forward_step, 0)
-    take_cot(0)
     lax.fori_loop(n // 2, n, forward_step, 0)
 
     def slab_half(who):
@@ -324,7 +325,7 @@
     weigh(me)
     backward(me)
     for k in range(n - 1):
-        if k:
+        if k >= 2:
             take_cot(k)
         for copy in core_copies[k * CUTS:(k + 1) * CUTS]:
             copy.wait_recv()

time: 71.1 us -> 68.9 us (0.969)
  Pallas kernels: 65.4 us -> 63.1 us
    pallas_call x1, Pallas kernels: 65.4 us -> 63.1 us  [fused(): pl.pallas_call(functools.partial(fused_kernel, n), out_shape=[jax.ShapeDt...]
where the time goes in v3:
time: 68.9 us; the launch traced here: 68.7 us
  Pallas kernels  63.1 us (92%)
  other arithmetic  2.85 us (4%)
  local copies, waits for them, and re-layouts  2.04 us (3%)
    pallas_call x1, Pallas kernels, fused(): pl.pallas_call(functools.partial(fused_kernel, n), out_shape=[jax.ShapeDt...  63.1 us
    convert_element_type x1, other arithmetic, fused(): return (dq[None], dk[None], dv[None], gw.astype(full))  2.85 us
    unnamed x9, local copies, waits for them, and re-layouts  2.04 us

profile of v3, /device:TPU:0, one launch (start us, length us, event | category | flops | bytes accessed | tf_op | source)
XLA Modules:
  0.0 68.7 jit_solution(8682302362177356592)
XLA Ops:
  0.6 63.1 %shard_map.93 = (bf16[192,512]{1,0:T(8,128)(2,1)}, bf16[192,512]{1,0:T(8,128)(2,1)}, bf16[192,512]{1,0:T(8,128)(2,1)}, bf16[512,1024]{1,0:T(8,128)(2,1)}) custom-call(bf16[192,512]{1,0:T(8,128)(2,1)} %bitcast.8, bf16[192,512]{1,0:T(8,128)(2,1)} %bitcast.9, bf16[192,512]{1,0:T(8,128)(2,1)} %bitcast.10, s32[1,192]{1,0:T(1,128)} %utt_ref.1, ...), custom_call_target="tpu_custom_call" | custom-call | tf_op jit(solution)/shard_map/pallas_call | solution.py:396
  63.8 0.0 copy-start.2
  63.8 0.0 copy-start.1
  63.8 0.0 copy-start
  63.8 2.8 %convert_element_type.3 = f32[512,1024]{1,0:T(8,128)} convert(bf16[512,1024]{1,0:T(8,128)(2,1)} %get-tuple-element.11) | non-fusion elementwise | flops 524288 | bytes 3145728 | tf_op jit(solution)/shard_map/convert_element_type | solution.py:429
  66.7 0.0 copy-done.2
  66.7 0.7 copy.13
  67.3 0.0 copy-done.1
  67.3 0.7 copy.14
  68.0 0.0 copy-done
  68.0 0.7 copy.15
Async XLA Ops:
  63.8 2.9 %copy-start.2 = (bf16[192,512]{1,0:T(8,128)(2,1)S(1)}, bf16[192,512]{1,0:T(8,128)(2,1)}, u32[]{:S(2)}) copy-start(bf16[192,512]{1,0:T(8,128)(2,1)} %get-tuple-element.8) | copy-start | bytes 589828
  63.8 3.6 %copy-start.1 = (bf16[192,512]{1,0:T(8,128)(2,1)S(1)}, bf16[192,512]{1,0:T(8,128)(2,1)}, u32[]{:S(2)}) copy-start(bf16[192,512]{1,0:T(8,128)(2,1)} %get-tuple-element.9) | copy-start | bytes 589828
  63.8 4.2 %copy-start = (bf16[192,512]{1,0:T(8,128)(2,1)S(1)}, bf16[192,512]{1,0:T(8,128)(2,1)}, u32[]{:S(2)}) copy-start(bf16[192,512]{1,0:T(8,128)(2,1)} %get-tuple-element.10) | copy-start | bytes 589828

commit v4 on v3

--- a/solution.py
+++ b/solution.py
@@ -288,6 +288,8 @@
     dv_acc[...] = jnp.zeros_like(dv_acc)
     lax.fori_loop(0, n // 2, forward_step, 0)
     lax.fori_loop(n // 2, n, forward_step, 0)
+    for k in range(2, n - 1):
+        take_cot(k)
 
     def slab_half(who):
         return pl.ds(pl.multiple_of(who * HD, HD), HD)
@@ -325,8 +327,6 @@
     weigh(me)
     backward(me)
     for k in range(n - 1):
-        if k >= 2:
-            take_cot(k)
         for copy in core_copies[k * CUTS:(k + 1) * CUTS]:
             copy.wait_recv()
         weigh(order[k])

time: 68.9 us -> 67.7 us (0.983)
  Pallas kernels: 63.1 us -> 62 us
    pallas_call x1, Pallas kernels: 63.1 us -> 62 us  [fused(): pl.pallas_call(functools.partial(fused_kernel, n), out_shape=[jax.ShapeDt...]
where the time goes in v4:
time: 67.7 us; the launch traced here: 67.6 us
  Pallas kernels  62 us (92%)
  other arithmetic  2.85 us (4%)
  local copies, waits for them, and re-layouts  2.04 us (3%)
    pallas_call x1, Pallas kernels, fused(): pl.pallas_call(functools.partial(fused_kernel, n), out_shape=[jax.ShapeDt...  62 us
    convert_element_type x1, other arithmetic, fused(): return (dq[None], dk[None], dv[None], gw.astype(full))  2.85 us
    unnamed x9, local copies, waits for them, and re-layouts  2.04 us

profile of v4, /device:TPU:0, one launch (start us, length us, event | category | flops | bytes accessed | tf_op | source)
XLA Modules:
  0.0 67.6 jit_solution(6465594724275023703)
XLA Ops:
  0.6 62.0 %shard_map.93 = (bf16[192,512]{1,0:T(8,128)(2,1)}, bf16[192,512]{1,0:T(8,128)(2,1)}, bf16[192,512]{1,0:T(8,128)(2,1)}, bf16[512,1024]{1,0:T(8,128)(2,1)}) custom-call(bf16[192,512]{1,0:T(8,128)(2,1)} %bitcast.8, bf16[192,512]{1,0:T(8,128)(2,1)} %bitcast.9, bf16[192,512]{1,0:T(8,128)(2,1)} %bitcast.10, s32[1,192]{1,0:T(1,128)} %utt_ref.1, ...), custom_call_target="tpu_custom_call" | custom-call | tf_op jit(solution)/shard_map/pallas_call | solution.py:396
  62.7 0.0 copy-start.2
  62.7 0.0 copy-start.1
  62.7 0.0 copy-start
  62.7 2.8 %convert_element_type.3 = f32[512,1024]{1,0:T(8,128)} convert(bf16[512,1024]{1,0:T(8,128)(2,1)} %get-tuple-element.11) | non-fusion elementwise | flops 524288 | bytes 3145728 | tf_op jit(solution)/shard_map/convert_element_type | solution.py:429
  65.5 0.0 copy-done.2
  65.5 0.7 %copy.13 = bf16[1,192,512]{2,1,0:T(8,128)(2,1)} copy(bf16[1,192,512]{2,1,0:T(8,128)(2,1)S(1)} %bitcast.13) | data formatting | bytes 393216
  66.2 0.0 copy-done.1
  66.2 0.7 %copy.14 = bf16[1,192,512]{2,1,0:T(8,128)(2,1)} copy(bf16[1,192,512]{2,1,0:T(8,128)(2,1)S(1)} %bitcast.12) | data formatting | bytes 393216
  66.9 0.0 copy-done
  66.9 0.7 %copy.15 = bf16[1,192,512]{2,1,0:T(8,128)(2,1)} copy(bf16[1,192,512]{2,1,0:T(8,128)(2,1)S(1)} %bitcast.11) | data formatting | bytes 393216
Async XLA Ops:
  62.7 2.9 %copy-start.2 = (bf16[192,512]{1,0:T(8,128)(2,1)S(1)}, bf16[192,512]{1,0:T(8,128)(2,1)}, u32[]{:S(2)}) copy-start(bf16[192,512]{1,0:T(8,128)(2,1)} %get-tuple-element.8) | copy-start | bytes 589828
  62.7 3.6 %copy-start.1 = (bf16[192,512]{1,0:T(8,128)(2,1)S(1)}, bf16[192,512]{1,0:T(8,128)(2,1)}, u32[]{:S(2)}) copy-start(bf16[192,512]{1,0:T(8,128)(2,1)} %get-tuple-element.9) | copy-start | bytes 589828
  62.7 4.2 %copy-start = (bf16[192,512]{1,0:T(8,128)(2,1)S(1)}, bf16[192,512]{1,0:T(8,128)(2,1)}, u32[]{:S(2)}) copy-start(bf16[192,512]{1,0:T(8,128)(2,1)} %get-tuple-element.10) | copy-start | bytes 589828
